TPU v7x, 32 devices: a whole 2x2x4 slice. The times are simulated.
32 devices in a mesh: freq: 2 (over x), row: 2 (over y), col: 8 (over z, core).
Axes of the slice: x: 2, y: 2, z: 4, core: 2. Of those that a mesh axis runs over, the one named last changes fastest.
Arguments:
- eps_slab: bfloat16 [4096, 30720], P(('freq', 'row'), 'col'), parts along dimension 0, may hold values from -0.03125 to 0.03125
- matrix_elements: bfloat16 [512, 30720], P('col'), may hold values from -6 to 6
- band_energy: float32 [512], replicated, may hold values from -2 to 2
- frequency: float32 [2], P('freq'), parts along dimension 0, may hold values from -1 to 1
Outputs:
- sigma: float32 [1024, 512], P(('freq', 'col'), 'row'), parts along dimension 0
There are 2 independent parts, one for each index of `freq`. A program takes and returns all parts, laid end to end along the dimension named above; an argument that names none is the same for every part. Nothing has to cross between parts.
All inputs are finite; a program needn't handle non-finite values.
Results may differ from a plain program's by a relative error of at most 0.0003.
Values may be sent and summed in bfloat16 or wider, within the bound.
A program may use at most 64 MiB of HBM per device.

v0:
```python
import math

import jax
import jax.numpy as jnp
from jax import lax
from jax.sharding import PartitionSpec as P


def shards(eps_slab, matrix_elements, band_energy, frequency):
    rows_dev = eps_slab.shape[0]
    cols_dev = eps_slab.shape[1]
    panel_width = matrix_elements.shape[0]
    col_count = lax.axis_size("col")
    row_count = lax.axis_size("row")
    pair_count = panel_width * col_count
    factor = 1.0 / math.sqrt(rows_dev * row_count)
    own_rows = lax.dynamic_slice_in_dim(
        matrix_elements, lax.axis_index("row") * rows_dev, rows_dev, 1
    )
    slab_block = lax.all_gather(own_rows, "col", axis=0, tiled=True)
    weight = 1.0 / (1.0 + (frequency[0] - band_energy) ** 2)
    weighted = slab_block.astype(jnp.float32) * (weight * factor)[:, None]
    grouped = matrix_elements.reshape(panel_width, col_count, cols_dev)
    screened_t = jnp.einsum(
        "jpg,rg->pjr",
        lax.all_to_all(grouped, "col", split_axis=1, concat_axis=1, tiled=True),
        eps_slab,
        preferred_element_type=jnp.float32,
    )
    screened_t = screened_t.reshape(pair_count, rows_dev)
    screened_block = lax.psum_scatter(screened_t, "col", scatter_dimension=0, tiled=True)
    partial_sigma = lax.dot_general(
        screened_block,
        weighted,
        (((1,), (1,)), ((), ())),
        precision=lax.Precision.HIGHEST,
        preferred_element_type=jnp.float32,
    )
    return lax.psum_scatter(partial_sigma, "row", scatter_dimension=1, tiled=True)


def solution(mesh):
    in_specs = (P(("freq", "row"), "col"), P("col", None), P(), P("freq"))
    out_specs = P(("freq", "col"), "row")
    return jax.shard_map(shards, mesh=mesh, in_specs=in_specs, out_specs=out_specs, check_vma=False)
```

profile of v0, /device:TPU:0, one launch (start us, length us, event | category | flops | bytes accessed | tf_op | source)
XLA Modules:
  0.0 178.5 jit_solution(11635007336402004960)
XLA Ops:
  6.5 4.3 %copy.8 = bf16[8,8,8,3840]{3,2,0,1:T(8,128)(2,1)} copy(bf16[8,8,8,3840]{3,2,1,0:T(8,128)(2,1)} %bitcast.15) | data formatting | bytes 7864320 | tf_op jit(solution)/shard_map/reshape | solution.py:23
  10.8 6.3 %all-to-all-start = ((bf16[64,8,3840]{2,0,1:T(8,128)(2,1)}), bf16[64,8,3840]{2,0,1:T(8,128)(2,1)}, u32[]{:S(2)}, u32[]{:S(2)}) async-start(bf16[64,8,3840]{2,0,1:T(8,128)(2,1)} %bitcast.14), calls=%async_computation | async-start | bytes 7864320 | tf_op jit(solution)/shard_map/all_to_all | solution.py:26
  17.1 0.0 all-gather.2.cloned.1.call-start
  17.2 1.6 constant_dynamic-slice_fusion
  18.8 0.0 all-gather.2.cloned.1.call-update
  18.8 0.0 copy-start
  18.8 0.0 reduce-scatter.3.cloned.1.call-start
  18.9 95.2 %all-to-all-done = bf16[64,8,3840]{2,0,1:T(8,128)(2,1)} async-done(((bf16[64,8,3840]{2,0,1:T(8,128)(2,1)}), bf16[64,8,3840]{2,0,1:T(8,128)(2,1)}, u32[]{:S(2)}, u32[]{:S(2)}) %all-to-all-start) | async-done | bytes 3932192 | tf_op jit(solution)/shard_map/all_to_all | solution.py:26
  114.1 9.9 %fusion = f32[1024,64,8]{0,1,2:T(8,128)} fusion(bf16[64,8,3840]{2,0,1:T(8,128)(2,1)} %all-to-all-done, bf16[1024,3840]{1,0:T(8,128)(2,1)} %param.4), kind=kOutput, calls=%fused_computation | convolution fusion | flops 4026531840 | bytes 13893632 | tf_op jit(solution)/shard_map/jpg,rg->pjr/dot_general | solution.py:24
  124.0 0.0 reduce-scatter.3.cloned.1.call-update
  124.0 0.0 reduce-scatter.5.cloned.1.call-start
  124.7 0.0 copy-done
  124.8 0.0 all-gather.2.cloned.1.call-done
  124.8 34.1 %reduce-scatter.3.cloned.1.call-done = f32[64,1024]{1,0:T(8,128)} async-done(((f32[512,1024]{1,0:T(8,128)}), f32[64,1024]{1,0:T(8,128)}) %reduce-scatter.3.cloned.1.call-update) | async-done | bytes 262160 | tf_op jit(solution)/shard_map/reduce_scatter | solution.py:31
  158.9 4.1 %fusion.2 = f32[64,512]{1,0:T(8,128)} fusion(f32[64,1024]{1,0:T(8,128)} %reduce-scatter.3.cloned.1.call-done, bf16[512,1024]{1,0:T(8,128)(2,1)} %all-gather.2.cloned.1.call-done, f32[512]{0:T(512)S(1)} %divide_multiply_fusion), kind=kOutput, calls=%fused_computation.3 | convolution fusion | flops 403701760 | bytes 1443840 | tf_op jit(solution)/shard_map/dot_general | solution.py:32
  163.0 0.0 reduce-scatter.5.cloned.1.call-update
  163.0 9.0 %reduce-scatter.5.cloned.1.call-done = f32[64,256]{1,0:T(8,128)} async-done(((f32[64,512]{1,0:T(8,128)}), f32[64,256]{1,0:T(8,128)}) %reduce-scatter.5.cloned.1.call-update) | async-done | bytes 65552 | tf_op jit(solution)/shard_map/reduce_scatter | solution.py:39
  (1 shorter events, 0.0 us)
Async XLA Ops:
  10.8 103.2 %all-to-all-start = ((bf16[64,8,3840]{2,0,1:T(8,128)(2,1)}), bf16[64,8,3840]{2,0,1:T(8,128)(2,1)}, u32[]{:S(2)}, u32[]{:S(2)}) async-start(bf16[64,8,3840]{2,0,1:T(8,128)(2,1)} %bitcast.14), calls=%async_computation | async-start | bytes 7864320 | tf_op jit(solution)/shard_map/all_to_all | solution.py:26
  17.1 107.6 %all-gather.2.cloned.1.call-start = ((), (), s32[]{:S(2)}) async-start(), calls=%async_computation.4 | async-start | bytes 1179648 | tf_op jit(solution)/shard_map/all_gather | solution.py:20
  18.8 105.9 %copy-start = (f32[512]{0:T(512)S(1)}, f32[512]{0:T(512)}, u32[]{:S(2)}) copy-start(f32[512]{0:T(512)} %param.6) | copy-start | bytes 6148
  18.8 140.1 %reduce-scatter.3.cloned.1.call-start = ((), (), s32[]{:S(2)}) async-start(), calls=%async_computation.3 | async-start | bytes 2359296 | tf_op jit(solution)/shard_map/reduce_scatter | solution.py:31
  124.0 48.0 %reduce-scatter.5.cloned.1.call-start = ((), (), s32[]{:S(2)}) async-start(), calls=%async_computation.5 | async-start | bytes 196608 | tf_op jit(solution)/shard_map/reduce_scatter | solution.py:39
Sparse Core Ops, SparseCore 0:
  19.6 34.0 all-gather.1
  124.2 34.6 reduce-scatter.2
  163.2 8.8 reduce-scatter.4
where the time goes:
time: 179 us
  waiting for transfers between devices  138 us (77%)
  matrix products  14.1 us (8%)
  between operations  13.8 us (8%)
  starting transfers between devices  6.45 us (4%)
  local copies, waits for them, and re-layouts  5.87 us (3%)
    all_to_all x1, waiting for transfers between devices, shards(): lax.all_to_all(grouped, 'col', split_axis=1, concat_axis=1, tiled=True)  95.2 us
    reduce_scatter x1, waiting for transfers between devices, shards(): lax.psum_scatter(screened_t, 'col', scatter_dimension=0, tiled=True)  34.1 us
    dot_general x1, matrix products, shards(): jnp.einsum('jpg,rg->pjr', lax.all_to_all(grouped, 'col', split_axis=1, co...  9.94 us
    reduce_scatter x1, waiting for transfers between devices, shards(): lax.psum_scatter(partial_sigma, 'row', scatter_dimension=1, tiled=True)  8.98 us
    all_to_all x1, starting transfers between devices, shards(): lax.all_to_all(grouped, 'col', split_axis=1, concat_axis=1, tiled=True)  6.33 us
    reshape x1, local copies, waits for them, and re-layouts, shards(): grouped = matrix_elements.reshape(panel_width, col_count, cols_dev)  4.28 us
    dot_general x1, matrix products, shards(): lax.dot_general(screened_block, weighted, (((1,), (1,)), ((), ())), preci...  4.12 us
  transfers between devices with their start and end apart: 4, of which 3 were waited for; matrix products, arithmetic and copies ran while one was open for 6% of the time, Pallas kernels for 0%

commit v1 on v0

v1 whole, which is shorter than its diff:
```python
import functools
import math

import jax
import jax.numpy as jnp
from jax import lax
from jax.experimental import pallas as pl
from jax.experimental.pallas import tpu as pltpu
from jax.sharding import PartitionSpec as P

MESH = pl.DeviceIdType.MESH
F32 = jnp.float32
BF16 = jnp.bfloat16


def flip(index, mask):
    bit = 1
    while bit <= mask:
        if mask & bit:
            index = index + bit * (1 - 2 * lax.rem(index // bit, 2))
        bit *= 2
    return index


def kernel(
    dims,
    eps_hbm, m_hbm, band_ref, freq_ref, out_ref,
    eps_v, slab, mbuf, thi, tlo, part, sib, qsum, yrecv, rsum, zrecv,
    local_sem, slab_send, slab_recv, m_send, m_recv,
    sib_send, sib_recv, y_send, y_recv, z_send, z_recv,
):
    n_row, n_col, rows, width, pw = dims
    n_chip = n_col // 2
    pairs = n_col * pw
    quarter = pw // 4
    n_half = pairs // n_row
    left_cols = -(-width // 256) * 128
    right_cols = width - left_cols

    f = lax.axis_index("freq")
    r = lax.axis_index("row")
    c = lax.axis_index("col")
    o = lax.rem(c, 2)
    parity = lax.rem(r, 2)
    xf = 1 - f
    yr = r + 1 - 2 * parity
    me = (f, r, c)
    x_dev = (xf, r, c)
    y_dev = (f, yr, c)
    sib_dev = (f, r, flip(c, 1))

    def rows_of(panel, first, count):
        return pl.ds(pl.multiple_of(panel * pw + first, 16), count)

    def cols_of(index, size):
        return pl.ds(pl.multiple_of(index * size, 128), size)

    load_eps = pltpu.make_async_copy(eps_hbm, eps_v, local_sem.at[0])
    load_eps.start()
    load_slab = pltpu.make_async_copy(
        m_hbm.at[:, cols_of(r, rows)], slab.at[rows_of(c, 0, pw)], local_sem.at[1])
    load_slab.start()
    load_m = pltpu.make_async_copy(
        m_hbm.at[:, cols_of(c, width)], mbuf.at[rows_of(c, 0, pw)], local_sem.at[2])
    load_m.start()

    barrier = pltpu.get_barrier_semaphore()
    for d in range(1, n_col):
        pl.semaphore_signal(barrier, inc=1, device_id=(f, r, flip(c, d)), device_id_type=MESH)
    pl.semaphore_signal(barrier, inc=1, device_id=x_dev, device_id_type=MESH)
    for dr in range(1, n_row):
        pl.semaphore_signal(barrier, inc=1, device_id=(f, lax.rem(r + dr, n_row), c), device_id_type=MESH)
    pl.semaphore_wait(barrier, n_col - 1 + 1 + n_row - 1)

    def copy(src, dst, send, recv, device):
        return pltpu.make_async_remote_copy(
            src_ref=src, dst_ref=dst, send_sem=send, recv_sem=recv,
            device_id=device, device_id_type=MESH)

    pending = []

    def start(desc):
        desc.start()
        pending.append(desc)

    def arrived(dst, recv):
        copy(dst, dst, recv, recv, me).wait_recv()

    chip_order = list(range(1, n_chip))
    remote = [2 * dk + dc for dk in chip_order for dc in range(2)]

    start(copy(m_hbm.at[:, cols_of(r, rows)], slab.at[rows_of(c, 0, pw)],
               slab_send.at[0, 1], slab_recv.at[0, 1], sib_dev))
    for d in remote:
        to = flip(c, d)
        q = quarter * (2 * f + lax.rem(to, 2))
        start(copy(m_hbm.at[pl.ds(pl.multiple_of(q, 16), quarter), cols_of(r, rows)],
                   slab.at[rows_of(c, q, quarter)],
                   slab_send.at[0, d], slab_recv.at[0, d], (f, r, to)))
    start(copy(m_hbm.at[:, cols_of(flip(c, 1), width)], mbuf.at[rows_of(c, 0, pw)],
               m_send.at[0, 1], m_recv.at[0, 1], sib_dev))
    mq = quarter * (2 * f + parity)
    mq_x = quarter * (2 * xf + parity)
    mq_y = quarter * (2 * f + 1 - parity)
    mq_d = quarter * (2 * xf + 1 - parity)
    for d in remote:
        to = flip(c, d)
        start(copy(m_hbm.at[pl.ds(pl.multiple_of(mq, 16), quarter), cols_of(to, width)],
                   mbuf.at[rows_of(c, mq, quarter)],
                   m_send.at[0, d], m_recv.at[0, d], (f, r, to)))

    sq = quarter * (2 * f + o)
    sq_x = quarter * (2 * xf + o)
    sq_s = quarter * (2 * f + 1 - o)
    sq_d = quarter * (2 * xf + 1 - o)
    for d in remote:
        own = slab.at[rows_of(flip(c, d), sq, quarter)]
        arrived(own, slab_recv.at[0, d])
        start(copy(own, own, slab_send.at[1, d], slab_recv.at[1, d], x_dev))
        start(copy(own, own, slab_send.at[2, d], slab_recv.at[2, d ^ 1], sib_dev))
    for d in remote:
        got = slab.at[rows_of(flip(c, d), sq_x, quarter)]
        arrived(got, slab_recv.at[1, d])
        start(copy(got, got, slab_send.at[3, d], slab_recv.at[3, d ^ 1], sib_dev))
    load_slab.wait()
    arrived(slab.at[rows_of(flip(c, 1), 0, pw)], slab_recv.at[0, 1])
    for d in remote:
        panel = flip(c, d)
        arrived(slab.at[rows_of(panel, sq_s, quarter)], slab_recv.at[2, d])
        arrived(slab.at[rows_of(panel, sq_d, quarter)], slab_recv.at[3, d])
    load_eps.wait()

    t_cols = 256 if width % 256 == 0 else 128
    t_steps = width // t_cols

    def t_range(first, last):
        @pl.loop(first, last)
        def _(step):
            cols = cols_of(step, t_cols)
            t = jnp.dot(slab[...], eps_v[:, cols], preferred_element_type=F32)
            hi = t.astype(BF16)
            thi[:, cols] = hi
            tlo[:, cols] = (t - hi.astype(F32)).astype(BF16)

    lcols = pl.ds(0, left_cols)
    rcols = pl.ds(left_cols, right_cols)

    def forward_first(dk):
        for d in (2 * dk, 2 * dk + 1):
            own = mbuf.at[rows_of(flip(c, d), mq, quarter)]
            arrived(own, m_recv.at[0, d])
            start(copy(own, own, m_send.at[1, d], m_recv.at[1, d], x_dev))
            start(copy(own, own, m_send.at[2, d], m_recv.at[2, d], y_dev))

    def forward_second(dk):
        for d in (2 * dk, 2 * dk + 1):
            from_x = mbuf.at[rows_of(flip(c, d), mq_x, quarter)]
            from_y = mbuf.at[rows_of(flip(c, d), mq_y, quarter)]
            arrived(from_x, m_recv.at[1, d])
            half = from_x.at[:, lcols]
            start(copy(half, half, m_send.at[3, d], m_recv.at[3, d], y_dev))
            arrived(from_y, m_recv.at[2, d])
            half = from_y.at[:, rcols]
            start(copy(half, half, m_send.at[4, d], m_recv.at[4, d], x_dev))

    k_cols = width // 5 if width % 640 == 0 else 128
    k_steps = width // k_cols

    def product(dk):
        for d in (2 * dk, 2 * dk + 1):
            panel = flip(c, d)
            if d == 0:
                load_m.wait()
            elif d == 1:
                arrived(mbuf.at[rows_of(panel, 0, pw)], m_recv.at[0, 1])
            else:
                diag = mbuf.at[rows_of(panel, mq_d, quarter)]
                arrived(diag.at[:, lcols], m_recv.at[3, d])
                arrived(diag.at[:, rcols], m_recv.at[4, d])
        chip_rows = pl.ds(pl.multiple_of(flip(c, 2 * dk) // 2 * (2 * pw), 2 * pw), 2 * pw)
        part[dk] = jnp.zeros((2 * pw, pairs), F32)

        @pl.loop(0, k_steps)
        def _(step):
            cols = cols_of(step, k_cols)
            m = mbuf[chip_rows, cols]
            nt = (((1,), (1,)), ((), ()))
            part[dk] += (
                lax.dot_general(m, thi[:, cols], nt, preferred_element_type=F32)
                + lax.dot_general(m, tlo[:, cols], nt, preferred_element_type=F32))

        theirs = part.at[dk, pl.ds(pl.multiple_of((1 - o) * pw, pw), pw)]
        start(copy(theirs, sib.at[dk], sib_send.at[dk], sib_recv.at[dk], sib_dev))

    def add_sibling(dk):
        arrived(sib.at[dk], sib_recv.at[dk])
        qsum[dk] = part[dk, pl.ds(pl.multiple_of(o * pw, pw), pw)] + sib[dk]
        for dr in range(1, n_row):
            to = lax.rem(r + dr, n_row)
            start(copy(qsum.at[dk, :, cols_of(to, n_half)], yrecv.at[dk, dr - 1],
                       y_send.at[dk, dr - 1], y_recv.at[dk, dr - 1], (f, to, c)))

    def add_rows(dk):
        total = qsum[dk, :, cols_of(r, n_half)]
        for dr in range(1, n_row):
            arrived(yrecv.at[dk, dr - 1], y_recv.at[dk, dr - 1])
            total += yrecv[dk, dr - 1]
        rsum[dk] = total
        if dk:
            start(copy(rsum.at[dk], zrecv.at[dk], z_send.at[dk], z_recv.at[dk],
                       (f, r, flip(c, 2 * dk))))

    first = chip_order[0]
    third = t_steps // 3
    t_range(0, third)
    forward_first(first)
    t_range(third, 2 * third)
    forward_second(first)
    t_range(2 * third, t_steps)
    done = 0
    product(0)
    for dk in chip_order[1:]:
        forward_first(dk)
        add_sibling(done)
        forward_second(dk)
        add_rows(done)
        done = chip_order[chip_order.index(dk) - 1]
        product(done)
    add_sibling(done)
    last = chip_order[-1]
    if last != done:
        add_rows(done)
        product(last)
        add_sibling(last)
    add_rows(last)

    total = rsum[0]
    for dk in chip_order:
        arrived(zrecv.at[dk], z_recv.at[dk])
        total += zrecv[dk]
    band = band_ref[:, cols_of(r, n_half)]
    weight = 1.0 / (1.0 + (freq_ref[0] - band) ** 2)
    out_ref[...] = total * (weight * (1.0 / math.sqrt(rows * n_row)))
    for desc in pending:
        desc.wait_send()


def shards(eps_slab, matrix_elements, band_energy, frequency):
    rows, width = eps_slab.shape
    pw = matrix_elements.shape[0]
    n_col = lax.axis_size("col")
    n_row = lax.axis_size("row")
    n_chip = n_col // 2
    pairs = pw * n_col
    n_half = pairs // n_row
    dma = pltpu.SemaphoreType.DMA
    hbm = pl.BlockSpec(memory_space=pl.ANY)
    return pl.pallas_call(
        functools.partial(kernel, (n_row, n_col, rows, width, pw)),
        out_shape=jax.ShapeDtypeStruct((pw, n_half), F32),
        in_specs=[hbm, hbm, pl.BlockSpec(memory_space=pltpu.VMEM), pl.BlockSpec(memory_space=pltpu.SMEM)],
        out_specs=pl.BlockSpec(memory_space=pltpu.VMEM),
        scratch_shapes=[
            pltpu.VMEM((rows, width), BF16),
            pltpu.VMEM((pairs, rows), BF16),
            pltpu.VMEM((pairs, width), BF16),
            pltpu.VMEM((pairs, width), BF16),
            pltpu.VMEM((pairs, width), BF16),
            pltpu.VMEM((n_chip, 2 * pw, pairs), F32),
            pltpu.VMEM((n_chip, pw, pairs), F32),
            pltpu.VMEM((n_chip, pw, pairs), F32),
            pltpu.VMEM((n_chip, n_row - 1, pw, n_half), F32),
            pltpu.VMEM((n_chip, pw, n_half), F32),
            pltpu.VMEM((n_chip, pw, n_half), F32),
            dma((3,)),
            dma((4, n_col)), dma((4, n_col)),
            dma((5, n_col)), dma((5, n_col)),
            dma((n_chip,)), dma((n_chip,)),
            dma((n_chip, n_row - 1)), dma((n_chip, n_row - 1)),
            dma((n_chip,)), dma((n_chip,)),
        ],
        compiler_params=pltpu.CompilerParams(
            collective_id=0, has_side_effects=True, vmem_limit_bytes=56 * 2 ** 20),
        cost_estimate=pl.CostEstimate(
            flops=2 * pairs * width * (rows + 2 * pairs),
            bytes_accessed=2 * rows * width + 2 * pw * width * n_col, transcendentals=0),
    )(eps_slab, matrix_elements, band_energy.reshape(1, pairs), frequency)


def solution(mesh):
    in_specs = (P(("freq", "row"), "col"), P("col", None), P(), P("freq"))
    out_specs = P(("freq", "col"), "row")
    return jax.shard_map(shards, mesh=mesh, in_specs=in_specs, out_specs=out_specs, check_vma=False)
```

time: 179 us -> 77.8 us (0.43)
  waiting for transfers between devices: 138 us -> 0 us
  Pallas kernels: 0 us -> 75.5 us
  matrix products: 14.1 us -> 0 us
  between operations: 13.8 us -> 0.66 us
  starting transfers between devices: 6.45 us -> 0 us
  local copies, waits for them, and re-layouts: 5.87 us -> 1.47 us
    all_to_all x1 -> x0, waiting for transfers between devices: 95.2 us -> none  [shards(): lax.all_to_all(grouped, 'col', split_axis=1, concat_axis=1, tiled=True)]
    pallas_call x0 -> x1, Pallas kernels: none -> 75.5 us  [shards(): pl.pallas_call(functools.partial(kernel, (n_row, n_col, rows, width, pw))...]
    reduce_scatter x2 -> x0, waiting for transfers between devices: 43.1 us -> none  [the longest x1 34.1 us: shards(): lax.psum_scatter(screened_t, 'col', scatter_dimension=0, tiled=True)]
    dot_general x2 -> x0, matrix products: 14.1 us -> none  [the longest x1 9.94 us: shards(): jnp.einsum('jpg,rg->pjr', lax.all_to_all(grouped, 'col', split_axis=1, co...]
    all_to_all x1 -> x0, starting transfers between devices: 6.33 us -> none  [shards(): lax.all_to_all(grouped, 'col', split_axis=1, concat_axis=1, tiled=True)]
    reshape x1 -> x0, local copies, waits for them, and re-layouts: 4.28 us -> none  [shards(): grouped = matrix_elements.reshape(panel_width, col_count, cols_dev)]
  transfers between devices with their start and end apart: 4 -> 0, of which waited for: 3 -> 0; matrix products, arithmetic and copies ran while one was open for 6% -> 0% of each run, Pallas kernels for 0% -> 0%
where the time goes in v1:
time: 77.8 us; the launch traced here: 77.6 us
  Pallas kernels  75.5 us (97%)
  local copies, waits for them, and re-layouts  1.47 us (2%)
    pallas_call x1, Pallas kernels, shards(): pl.pallas_call(functools.partial(kernel, (n_row, n_col, rows, width, pw))...  75.5 us

profile of v1, /device:TPU:0, one launch (start us, length us, event | category | flops | bytes accessed | tf_op | source)
XLA Modules:
  0.0 77.6 jit_solution(15435985196042124719)
XLA Ops:
  0.7 75.5 %shard_map.46 = f32[64,256]{1,0:T(8,128)} custom-call(bf16[1024,3840]{1,0:T(8,128)(2,1)} %eps_hbm.1, bf16[64,30720]{1,0:T(8,128)(2,1)} %m_hbm.1, f32[1,512]{1,0:T(1,128)} %bitcast.1, f32[1]{0:T(128)S(6)} %copy.6.freq_ref), custom_call_target="tpu_custom_call" | custom-call | flops 8053063680 | bytes 11796480 | tf_op jit(solution)/shard_map/pallas_call | solution.py:258
  76.2 1.5 %copy.7 = f32[64,256]{1,0:T(8,128)} copy(f32[64,256]{1,0:T(8,128)} %shard_map.46) | data formatting | bytes 131072

commit v2 on v1

v2 whole, which is shorter than its diff:
```python
import functools
import math

import jax
import jax.numpy as jnp
from jax import lax
from jax.experimental import pallas as pl
from jax.experimental.pallas import tpu as pltpu
from jax.sharding import PartitionSpec as P

MESH = pl.DeviceIdType.MESH
F32 = jnp.float32
BF16 = jnp.bfloat16


def flip(index, mask):
    bit = 1
    while bit <= mask:
        if mask & bit:
            index = index + bit * (1 - 2 * lax.rem(index // bit, 2))
        bit *= 2
    return index


def kernel(
    dims,
    eps_hbm, m_hbm, band_ref, freq_ref, out_ref,
    eps_v, slab, mbuf, thi, tlo, part, sib, qsum, yrecv, rsum, zrecv,
    local_sem, slab_send, slab_recv, m_send, m_recv,
    sib_send, sib_recv, y_send, y_recv, z_send, z_recv,
):
    n_row, n_col, rows, width, pw, stages = dims
    n_chip = n_col // 2
    pairs = n_col * pw
    quarter = pw // 4
    n_half = pairs // n_row

    f = lax.axis_index("freq")
    r = lax.axis_index("row")
    c = lax.axis_index("col")
    o = lax.rem(c, 2)
    parity = lax.rem(r, 2)
    xf = 1 - f
    yr = r + 1 - 2 * parity
    me = (f, r, c)
    x_dev = (xf, r, c)
    y_dev = (f, yr, c)
    sib_dev = (f, r, flip(c, 1))

    def rows_of(panel, first, count):
        return pl.ds(pl.multiple_of(panel * pw + first, 16), count)

    def cols_of(index, size):
        return pl.ds(pl.multiple_of(index * size, 128), size)

    load_eps = pltpu.make_async_copy(eps_hbm, eps_v, local_sem.at[0])
    load_eps.start()
    load_slab = pltpu.make_async_copy(
        m_hbm.at[:, cols_of(r, rows)], slab.at[rows_of(c, 0, pw)], local_sem.at[1])
    load_slab.start()
    load_m = pltpu.make_async_copy(
        m_hbm.at[:, cols_of(c, width)], mbuf.at[rows_of(c, 0, pw)], local_sem.at[2])
    load_m.start()

    barrier = pltpu.get_barrier_semaphore()
    for d in range(1, n_col):
        pl.semaphore_signal(barrier, inc=1, device_id=(f, r, flip(c, d)), device_id_type=MESH)
    pl.semaphore_signal(barrier, inc=1, device_id=x_dev, device_id_type=MESH)
    for dr in range(1, n_row):
        pl.semaphore_signal(barrier, inc=1, device_id=(f, lax.rem(r + dr, n_row), c), device_id_type=MESH)
    pl.semaphore_wait(barrier, n_col - 1 + 1 + n_row - 1)

    def copy(src, dst, send, recv, device):
        return pltpu.make_async_remote_copy(
            src_ref=src, dst_ref=dst, send_sem=send, recv_sem=recv,
            device_id=device, device_id_type=MESH)

    pending = []

    def start(desc):
        desc.start()
        pending.append(desc)

    def arrived(dst, recv):
        copy(dst, dst, recv, recv, me).wait_recv()

    far_first = list(range(n_chip - 1, 0, -1))
    remote = [2 * dk + dc for dk in far_first for dc in range(2)]
    k_cols = width // stages
    t_cols = 256 if k_cols % 256 == 0 else 128

    start(copy(m_hbm.at[:, cols_of(r, rows)], slab.at[rows_of(c, 0, pw)],
               slab_send.at[0, 1], slab_recv.at[0, 1], sib_dev))
    for d in remote:
        to = flip(c, d)
        q = quarter * (2 * f + lax.rem(to, 2))
        start(copy(m_hbm.at[pl.ds(pl.multiple_of(q, 16), quarter), cols_of(r, rows)],
                   slab.at[rows_of(c, q, quarter)],
                   slab_send.at[0, d], slab_recv.at[0, d], (f, r, to)))

    mq = quarter * (2 * f + parity)
    mq_x = quarter * (2 * xf + parity)
    mq_y = quarter * (2 * f + 1 - parity)
    mq_d = quarter * (2 * xf + 1 - parity)

    def block(panel, first, stage):
        return mbuf.at[rows_of(panel, first, quarter), pl.ds(stage * k_cols, k_cols)]

    def send_z(stage, d):
        to = flip(c, d)
        cols = pl.ds(pl.multiple_of(to * width + stage * k_cols, 128), k_cols)
        start(copy(m_hbm.at[pl.ds(pl.multiple_of(mq, 16), quarter), cols], block(c, mq, stage),
                   m_send.at[0, stage, d], m_recv.at[0, stage, d], (f, r, to)))

    def forward_first(stage):
        for d in remote:
            own = block(flip(c, d), mq, stage)
            arrived(own, m_recv.at[0, stage, d])
            start(copy(own, own, m_send.at[1, stage, d], m_recv.at[1, stage, d], x_dev))
            start(copy(own, own, m_send.at[2, stage, d], m_recv.at[2, stage, d], y_dev))
            if stage + 2 < stages:
                send_z(stage + 2, d)

    def forward_second(stage):
        for d in remote:
            panel = flip(c, d)
            from_x, from_y = block(panel, mq_x, stage), block(panel, mq_y, stage)
            arrived(from_x, m_recv.at[1, stage, d])
            arrived(from_y, m_recv.at[2, stage, d])
            if d % 2 == 0:
                start(copy(from_x, from_x, m_send.at[3, stage, d], m_recv.at[3, stage, d], y_dev))
            else:
                start(copy(from_y, from_y, m_send.at[3, stage, d], m_recv.at[3, stage, d], x_dev))

    def t_chunk(stage):
        @pl.loop(0, k_cols // t_cols)
        def _(step):
            cols = pl.ds(pl.multiple_of(stage * k_cols + step * t_cols, 128), t_cols)
            t = jnp.dot(slab[...], eps_v[:, cols], preferred_element_type=F32)
            hi = t.astype(BF16)
            thi[:, cols] = hi
            tlo[:, cols] = (t - hi.astype(F32)).astype(BF16)

    def wait_chunk(stage):
        for d in remote:
            arrived(block(flip(c, d), mq_d, stage), m_recv.at[3, stage, d])
        if stage == 0:
            load_m.wait()
            arrived(mbuf.at[rows_of(flip(c, 1), 0, pw)], m_recv.at[0, 0, 1])

    n_cols = 256 if pairs % 256 == 0 else 128

    def product(stage, m_rows):
        cols = pl.ds(stage * k_cols, k_cols)
        nt = (((1,), (1,)), ((), ()))

        @pl.loop(0, pairs // n_cols)
        def _(step):
            ns = pl.ds(pl.multiple_of(step * n_cols, n_cols), n_cols)
            m = mbuf[m_rows, cols]
            p = (lax.dot_general(m, thi[ns, cols], nt, preferred_element_type=F32)
                 + lax.dot_general(m, tlo[ns, cols], nt, preferred_element_type=F32))
            out_cols = pl.ds(pl.multiple_of(step * n_cols, n_cols), n_cols)
            if stage:
                part[m_rows, out_cols] += p
            else:
                part[m_rows, out_cols] = p

    def panel_rows(dk, core):
        return rows_of(2 * (flip(c, 2 * dk) // 2) + core, 0, pw)

    def send_sibling(dk):
        start(copy(part.at[panel_rows(dk, 1 - o)], sib.at[dk], sib_send.at[dk], sib_recv.at[dk], sib_dev))

    def add_sibling(dk):
        arrived(sib.at[dk], sib_recv.at[dk])
        qsum[dk] = part[panel_rows(dk, o), :] + sib[dk]
        for dr in range(1, n_row):
            to = lax.rem(r + dr, n_row)
            start(copy(qsum.at[dk, :, cols_of(to, n_half)], yrecv.at[dk, dr - 1],
                       y_send.at[dk, dr - 1], y_recv.at[dk, dr - 1], (f, to, c)))

    def add_rows(dk):
        total = qsum[dk, :, cols_of(r, n_half)]
        for dr in range(1, n_row):
            arrived(yrecv.at[dk, dr - 1], y_recv.at[dk, dr - 1])
            total += yrecv[dk, dr - 1]
        rsum[dk] = total
        if dk:
            start(copy(rsum.at[dk], zrecv.at[dk], z_send.at[dk], z_recv.at[dk],
                       (f, r, flip(c, 2 * dk))))

    for stage in range(min(2, stages)):
        for d in remote:
            send_z(stage, d)
    start(copy(m_hbm.at[:, cols_of(flip(c, 1), width)], mbuf.at[rows_of(c, 0, pw)],
               m_send.at[0, 0, 1], m_recv.at[0, 0, 1], sib_dev))

    sq = quarter * (2 * f + o)
    sq_x = quarter * (2 * xf + o)
    sq_s = quarter * (2 * f + 1 - o)
    sq_d = quarter * (2 * xf + 1 - o)
    for d in remote:
        own = slab.at[rows_of(flip(c, d), sq, quarter)]
        arrived(own, slab_recv.at[0, d])
        start(copy(own, own, slab_send.at[1, d], slab_recv.at[1, d], x_dev))
        start(copy(own, own, slab_send.at[2, d], slab_recv.at[2, d ^ 1], sib_dev))
    forward_first(0)
    for d in remote:
        got = slab.at[rows_of(flip(c, d), sq_x, quarter)]
        arrived(got, slab_recv.at[1, d])
        start(copy(got, got, slab_send.at[3, d], slab_recv.at[3, d ^ 1], sib_dev))
    forward_second(0)
    if stages > 1:
        forward_first(1)
    load_slab.wait()
    arrived(slab.at[rows_of(flip(c, 1), 0, pw)], slab_recv.at[0, 1])
    for d in remote:
        panel = flip(c, d)
        arrived(slab.at[rows_of(panel, sq_s, quarter)], slab_recv.at[2, d])
        arrived(slab.at[rows_of(panel, sq_d, quarter)], slab_recv.at[3, d])
    load_eps.wait()
    t_chunk(0)
    all_rows = pl.ds(0, pairs)
    for stage in range(stages - 1):
        forward_second(stage + 1)
        if stage + 2 < stages:
            forward_first(stage + 2)
        t_chunk(stage + 1)
        wait_chunk(stage)
        product(stage, all_rows)

    wait_chunk(stages - 1)
    order = far_first + [0]
    for i, dk in enumerate(order):
        product(stages - 1, rows_of(2 * (flip(c, 2 * dk) // 2), 0, 2 * pw))
        send_sibling(dk)
        if i >= 1:
            add_sibling(order[i - 1])
        if i >= 2:
            add_rows(order[i - 2])
    add_sibling(order[-1])
    for dk in order[-2:]:
        add_rows(dk)

    total = rsum[0]
    for dk in far_first:
        arrived(zrecv.at[dk], z_recv.at[dk])
        total += zrecv[dk]
    band = band_ref[:, cols_of(r, n_half)]
    weight = 1.0 / (1.0 + (freq_ref[0] - band) ** 2)
    out_ref[...] = total * (weight * (1.0 / math.sqrt(rows * n_row)))
    for desc in pending:
        desc.wait_send()


def shards(eps_slab, matrix_elements, band_energy, frequency):
    rows, width = eps_slab.shape
    pw = matrix_elements.shape[0]
    n_col = lax.axis_size("col")
    n_row = lax.axis_size("row")
    n_chip = n_col // 2
    pairs = pw * n_col
    n_half = pairs // n_row
    stages = next(n for n in (5, 4, 3, 2, 1) if width % (128 * n) == 0)
    dma = pltpu.SemaphoreType.DMA
    hbm = pl.BlockSpec(memory_space=pl.ANY)
    return pl.pallas_call(
        functools.partial(kernel, (n_row, n_col, rows, width, pw, stages)),
        out_shape=jax.ShapeDtypeStruct((pw, n_half), F32),
        in_specs=[hbm, hbm, pl.BlockSpec(memory_space=pltpu.VMEM), pl.BlockSpec(memory_space=pltpu.SMEM)],
        out_specs=pl.BlockSpec(memory_space=pltpu.VMEM),
        scratch_shapes=[
            pltpu.VMEM((rows, width), BF16),
            pltpu.VMEM((pairs, rows), BF16),
            pltpu.VMEM((pairs, width), BF16),
            pltpu.VMEM((pairs, width), BF16),
            pltpu.VMEM((pairs, width), BF16),
            pltpu.VMEM((pairs, pairs), F32),
            pltpu.VMEM((n_chip, pw, pairs), F32),
            pltpu.VMEM((n_chip, pw, pairs), F32),
            pltpu.VMEM((n_chip, n_row - 1, pw, n_half), F32),
            pltpu.VMEM((n_chip, pw, n_half), F32),
            pltpu.VMEM((n_chip, pw, n_half), F32),
            dma((3,)),
            dma((4, n_col)), dma((4, n_col)),
            dma((4, stages, n_col)), dma((4, stages, n_col)),
            dma((n_chip,)), dma((n_chip,)),
            dma((n_chip, n_row - 1)), dma((n_chip, n_row - 1)),
            dma((n_chip,)), dma((n_chip,)),
        ],
        compiler_params=pltpu.CompilerParams(
            collective_id=0, has_side_effects=True, vmem_limit_bytes=56 * 2 ** 20),
        cost_estimate=pl.CostEstimate(
            flops=2 * pairs * width * (rows + 2 * pairs),
            bytes_accessed=2 * rows * width + 2 * pw * width * n_col, transcendentals=0),
    )(eps_slab, matrix_elements, band_energy.reshape(1, pairs), frequency)


def solution(mesh):
    in_specs = (P(("freq", "row"), "col"), P("col", None), P(), P("freq"))
    out_specs = P(("freq", "col"), "row")
    return jax.shard_map(shards, mesh=mesh, in_specs=in_specs, out_specs=out_specs, check_vma=False)
```

time: 77.8 us -> 69.3 us (0.89)
  Pallas kernels: 75.5 us -> 67 us
    pallas_call x1, Pallas kernels: 75.5 us -> 67 us  [shards(): pl.pallas_call(functools.partial(kernel, (n_row, n_col, rows, width, pw,...]
where the time goes in v2:
time: 69.3 us; the launch traced here: 69.2 us
  Pallas kernels  67 us (97%)
  local copies, waits for them, and re-layouts  1.47 us (2%)
    pallas_call x1, Pallas kernels, shards(): pl.pallas_call(functools.partial(kernel, (n_row, n_col, rows, width, pw,...  67 us
    unnamed x1, local copies, waits for them, and re-layouts  1.47 us

profile of v2, /device:TPU:0, one launch (start us, length us, event | category | flops | bytes accessed | tf_op | source)
XLA Modules:
  0.0 69.2 jit_solution(9352927345733795939)
XLA Ops:
  0.7 67.0 %shard_map.46 = f32[64,256]{1,0:T(8,128)} custom-call(bf16[1024,3840]{1,0:T(8,128)(2,1)} %eps_hbm.1, bf16[64,30720]{1,0:T(8,128)(2,1)} %m_hbm.1, f32[1,512]{1,0:T(1,128)} %bitcast.1, f32[1]{0:T(128)S(6)} %copy.6.freq_ref), custom_call_target="tpu_custom_call" | custom-call | flops 8053063680 | bytes 11796480 | tf_op jit(solution)/shard_map/pallas_call | solution.py:268
  67.7 1.5 %copy.7 = f32[64,256]{1,0:T(8,128)} copy(f32[64,256]{1,0:T(8,128)} %shard_map.46) | data formatting | bytes 131072

commit v3 on v2

--- a/solution.py
+++ b/solution.py
@@ -125,11 +125,11 @@
         for d in remote:
             panel = flip(c, d)
             from_x, from_y = block(panel, mq_x, stage), block(panel, mq_y, stage)
-            arrived(from_x, m_recv.at[1, stage, d])
-            arrived(from_y, m_recv.at[2, stage, d])
             if d % 2 == 0:
+                arrived(from_x, m_recv.at[1, stage, d])
                 start(copy(from_x, from_x, m_send.at[3, stage, d], m_recv.at[3, stage, d], y_dev))
             else:
+                arrived(from_y, m_recv.at[2, stage, d])
                 start(copy(from_y, from_y, m_send.at[3, stage, d], m_recv.at[3, stage, d], x_dev))
 
     def t_chunk(stage):
@@ -143,7 +143,12 @@
 
     def wait_chunk(stage):
         for d in remote:
-            arrived(block(flip(c, d), mq_d, stage), m_recv.at[3, stage, d])
+            panel = flip(c, d)
+            if d % 2 == 0:
+                arrived(block(panel, mq_y, stage), m_recv.at[2, stage, d])
+            else:
+                arrived(block(panel, mq_x, stage), m_recv.at[1, stage, d])
+            arrived(block(panel, mq_d, stage), m_recv.at[3, stage, d])
         if stage == 0:
             load_m.wait()
             arrived(mbuf.at[rows_of(flip(c, 1), 0, pw)], m_recv.at[0, 0, 1])
@@ -210,9 +215,9 @@
         got = slab.at[rows_of(flip(c, d), sq_x, quarter)]
         arrived(got, slab_recv.at[1, d])
         start(copy(got, got, slab_send.at[3, d], slab_recv.at[3, d ^ 1], sib_dev))
-    forward_second(0)
     if stages > 1:
         forward_first(1)
+    forward_second(0)
     load_slab.wait()
     arrived(slab.at[rows_of(flip(c, 1), 0, pw)], slab_recv.at[0, 1])
     for d in remote:
@@ -223,9 +228,9 @@
     t_chunk(0)
     all_rows = pl.ds(0, pairs)
     for stage in range(stages - 1):
-        forward_second(stage + 1)
         if stage + 2 < stages:
             forward_first(stage + 2)
+        forward_second(stage + 1)
         t_chunk(stage + 1)
         wait_chunk(stage)
         product(stage, all_rows)

time: 69.3 us -> 66.1 us (0.954)
  Pallas kernels: 67 us -> 63.7 us
    pallas_call x1, Pallas kernels: 67 us -> 63.7 us  [shards(): pl.pallas_call(functools.partial(kernel, (n_row, n_col, rows, width, pw,...]
where the time goes in v3:
time: 66.1 us; the launch traced here: 65.9 us
  Pallas kernels  63.7 us (96%)
  local copies, waits for them, and re-layouts  1.47 us (2%)
    pallas_call x1, Pallas kernels, shards(): pl.pallas_call(functools.partial(kernel, (n_row, n_col, rows, width, pw,...  63.7 us
    unnamed x1, local copies, waits for them, and re-layouts  1.47 us

profile of v3, /device:TPU:0, one launch (start us, length us, event | category | flops | bytes accessed | tf_op | source)
XLA Modules:
  0.0 65.9 jit_solution(9406638845704810105)
XLA Ops:
  0.7 63.7 %shard_map.46 = f32[64,256]{1,0:T(8,128)} custom-call(bf16[1024,3840]{1,0:T(8,128)(2,1)} %eps_hbm.1, bf16[64,30720]{1,0:T(8,128)(2,1)} %m_hbm.1, f32[1,512]{1,0:T(1,128)} %bitcast.1, f32[1]{0:T(128)S(6)} %copy.6.freq_ref), custom_call_target="tpu_custom_call" | custom-call | flops 8053063680 | bytes 11796480 | tf_op jit(solution)/shard_map/pallas_call | solution.py:273
  64.4 1.5 %copy.7 = f32[64,256]{1,0:T(8,128)} copy(f32[64,256]{1,0:T(8,128)} %shard_map.46) | data formatting | bytes 131072
